TPU v7x, 256 devices: a whole 4x4x8 slice. The times are simulated.
256 devices in a mesh: replica: 4 (over y), fsdp: 64 (over z, x, core).
Axes of the slice: x: 4, y: 4, z: 8, core: 2. Of those that a mesh axis runs over, the one named last changes fastest.
Arguments:
- grads: bfloat16 [4, 64, 1024, 1024], P('replica', None, 'fsdp')
- block_owner: int32 [64], replicated, may hold values from 0 to 63, as said below
- left_roots: bfloat16 [128, 1024, 1024], P('fsdp')
- right_roots: bfloat16 [128, 1024, 1024], P('fsdp')
Outputs:
- direction: bfloat16 [64, 1024, 1024], P(None, 'fsdp')
Inputs may be any that keep to these rules, and one draw needn't show every extreme that they name: `block_owner`: each fsdp rank owns at most 2 blocks, and some rank owns exactly 2.
All inputs are finite; a program needn't handle non-finite values.
Results may differ from a plain program's by a relative error of at most 0.017.
Values may be sent and summed in bfloat16 or wider, within the bound.
A program may use at most 128 MiB of HBM per device.

v0:
```python
import jax
import jax.numpy as jnp
from jax import lax
from jax.sharding import PartitionSpec as P

EPSILON = 1e-06


def slot_ranks(block_owner):
    same_owner = block_owner[:, None] == block_owner[None, :]
    positions = jnp.arange(block_owner.shape[0], dtype=jnp.int32)
    earlier = positions[None, :] < positions[:, None]
    return jnp.sum(jnp.logical_and(same_owner, earlier).astype(jnp.int32), axis=1)


def on_device(grads, block_owner, left_roots, right_roots):
    rank_count = lax.axis_size("fsdp")
    slot_count = left_roots.shape[0]
    block_side = left_roots.shape[1]
    block_count = block_owner.shape[0]
    row_count = grads.shape[2]
    slot_rank = slot_ranks(block_owner)
    slot_keys = block_owner * slot_count + slot_rank
    home_keys = slot_rank * rank_count + block_owner
    matches = slot_keys[:, None] == jnp.arange(rank_count * slot_count, dtype=jnp.int32)[None, :]
    holder = jnp.sum(
        jnp.where(matches, jnp.arange(block_count, dtype=jnp.int32)[:, None], 0), axis=0
    )
    filled = jnp.any(matches, axis=0)
    holder = holder.reshape(rank_count, slot_count).T
    filled = filled.reshape(rank_count, slot_count).T
    partial_value = grads[0].astype(jnp.float32)
    shared = lax.psum(partial_value.astype(jnp.bfloat16), "replica")
    outgoing = jnp.where(
        filled[:, :, None, None], jnp.take(shared, holder, axis=0), jnp.zeros((), jnp.bfloat16)
    )
    arrived = lax.all_to_all(outgoing, "fsdp", split_axis=1, concat_axis=1, tiled=True)
    owned_blocks = arrived.reshape(slot_count, block_side, arrived.shape[3])
    grad_ms = jnp.mean(jnp.square(owned_blocks.astype(jnp.float32)), axis=(1, 2))
    middle = jnp.einsum(
        "sij,sjk->sik", left_roots, owned_blocks, preferred_element_type=jnp.float32
    ).astype(jnp.bfloat16)
    precond = jnp.einsum("sij,sjk->sik", middle, right_roots, preferred_element_type=jnp.float32)
    pre_ms = jnp.mean(jnp.square(precond), axis=(1, 2))
    factor = jnp.sqrt(grad_ms) * lax.rsqrt(pre_ms + EPSILON)
    updates = (precond * factor[:, None, None]).astype(jnp.bfloat16)
    updates = updates.reshape(slot_count, rank_count, row_count, block_side)
    returned = lax.all_to_all(updates, "fsdp", split_axis=1, concat_axis=1, tiled=True)
    return jnp.take(
        returned.reshape(slot_count * rank_count, row_count, block_side), home_keys, axis=0
    )


def solution(mesh):
    in_specs = (P("replica", None, "fsdp", None), P(), P("fsdp", None, None), P("fsdp", None, None))
    out_specs = P(None, "fsdp", None)
    return jax.shard_map(
        on_device, mesh=mesh, in_specs=in_specs, out_specs=out_specs, check_vma=False
    )
```

profile of v0, /device:TPU:1, one launch (start us, length us, event | category | flops | bytes accessed | tf_op | source)
XLA Modules:
  0.0 338.4 jit_solution(12886061774000895371)
XLA Ops:
  6.5 0.7 all-reduce.2.cloned.1.call-update
  7.3 0.9 convert_reduce_fusion
  8.2 0.7 multiply_add_fusion
  8.8 0.1 fusion.4
  8.9 0.2 reshape.39
  9.1 0.1 copy.25
  9.2 0.1 select_reduce_fusion
  9.3 0.1 reshape.40
  9.7 67.7 %all-reduce.2.cloned.1.call-done = bf16[64,16,1024]{2,1,0:T(8,128)(2,1)} async-done(((bf16[64,16,1024]{2,1,0:T(8,128)(2,1)}), bf16[64,16,1024]{2,1,0:T(8,128)(2,1)}) %all-reduce.2.cloned.1.call-update) | async-done | bytes 2097168 | tf_op jit(solution)/shard_map/psum | solution.py:33
  77.4 4.3 %gather_fusion = bf16[128,16,1024]{2,1,0:T(8,128)(2,1)} fusion(bf16[64,16,1024]{2,1,0:T(8,128)(2,1)} %all-reduce.2.cloned.1.call-done, s32[1024]{0:T(1024)S(1)} %pad_clamp_fusion.1), kind=kCustom, calls=%fused_computation | custom fusion | bytes 8389120 | tf_op jit(solution)/shard_map/jit(_take)/gather | solution.py:35
  81.7 2.6 select_select_fusion
  84.3 0.8 copy.28
  85.1 105.1 %all_to_all.10 = bf16[2,64,16,1024]{3,2,0,1:T(8,128)(2,1)S(1)} all-to-all(bf16[2,64,16,1024]{3,2,0,1:T(8,128)(2,1)S(1)} %copy.28), channel_id=1, replica_groups=mesh['replica'=4,'fsdp'=64] {'fsdp'}, dimensions={1} | all-to-all | bytes 8388608 | tf_op jit(solution)/shard_map/all_to_all | solution.py:37
  190.2 2.0 copy-done
  192.2 2.4 copy.29
  194.6 15.0 %multiply_reduce_fusion = (f32[2]{0:T(128)S(1)}, f32[2,1024,1024]{2,1,0:T(8,128)}) fusion(bf16[2,1024,1024]{2,1,0:T(8,128)(2,1)} %param.7, bf16[2,1024,1024]{2,1,0:T(8,128)(2,1)} %bitcast.16, bf16[2,1024,1024]{2,1,0:T(8,128)(2,1)} %param.6), kind=kOutput, calls=%fused_computation.3 | convolution fusion | flops 8596226048 | bytes 20971528 | tf_op jit(solution)/shard_map/sij,sjk->sik/dot_general | solution.py:43
  209.6 3.4 %multiply_reduce_fusion.1 = f32[2]{0:T(128)S(1)} fusion(bf16[2,64,16,1024]{3,2,0,1:T(8,128)(2,1)} %copy-done), kind=kLoop, calls=%fused_computation.4 | loop fusion | flops 6291454 | bytes 4194312 | tf_op jit(solution)/shard_map/reduce_sum | solution.py:39
  213.0 4.7 %multiply_convert_fusion = bf16[2,1024,1024]{2,1,0:T(8,128)(2,1)S(1)} fusion(f32[2,1024,1024]{2,1,0:T(8,128)} %get-tuple-element.8, f32[2]{0:T(128)S(1)} %rsqrt_multiply_fusion), kind=kLoop, calls=%fused_computation.2 | loop fusion | flops 4194304 | bytes 12582920 | tf_op jit(solution)/shard_map/convert_element_type | solution.py:46
  217.7 2.5 copy.32
  220.2 7.3 %all-to-all-start.1 = ((bf16[2,64,16,1024]{3,2,0,1:T(8,128)(2,1)}), bf16[2,64,16,1024]{3,2,0,1:T(8,128)(2,1)}, u32[]{:S(2)}, u32[]{:S(2)}) async-start(bf16[2,64,16,1024]{3,2,0,1:T(8,128)(2,1)} %copy.32), calls=%async_computation.1 | async-start | bytes 8388608 | tf_op jit(solution)/shard_map/all_to_all | solution.py:48
  227.6 94.5 %all-to-all-done.1 = bf16[2,64,16,1024]{3,2,0,1:T(8,128)(2,1)} async-done(((bf16[2,64,16,1024]{3,2,0,1:T(8,128)(2,1)}), bf16[2,64,16,1024]{3,2,0,1:T(8,128)(2,1)}, u32[]{:S(2)}, u32[]{:S(2)}) %all-to-all-start.1) | async-done | bytes 4194336 | tf_op jit(solution)/shard_map/all_to_all | solution.py:48
  322.1 5.0 %copy.33 = bf16[2,64,16,1024]{3,2,1,0:T(8,128)(2,1)} copy(bf16[2,64,16,1024]{3,2,0,1:T(8,128)(2,1)} %all-to-all-done.1) | data formatting | bytes 8388608 | tf_op jit(solution)/shard_map/all_to_all | solution.py:48
  327.1 2.9 gather_fusion.1
  330.0 1.6 broadcast_select_fusion
  (13 shorter events, 0.3 us)
Async XLA Ops:
  6.5 70.9 %all-reduce.2.cloned.1.call-start = ((), (), s32[]{:S(2)}) async-start(), calls=%async_computation.2 | async-start | bytes 4194304 | tf_op jit(solution)/shard_map/psum | solution.py:33
  190.2 2.0 copy-start
  220.2 7.4 %copy-start.1 = (s32[64]{0:T(128)S(1)}, s32[64]{0:T(128)}, u32[]{:S(2)}) copy-start(s32[64]{0:T(128)} %param.5) | copy-start | bytes 772
  220.2 101.9 %all-to-all-start.1 = ((bf16[2,64,16,1024]{3,2,0,1:T(8,128)(2,1)}), bf16[2,64,16,1024]{3,2,0,1:T(8,128)(2,1)}, u32[]{:S(2)}, u32[]{:S(2)}) async-start(bf16[2,64,16,1024]{3,2,0,1:T(8,128)(2,1)} %copy.32), calls=%async_computation.1 | async-start | bytes 8388608 | tf_op jit(solution)/shard_map/all_to_all | solution.py:48
Sparse Core Ops, SparseCore 0:
  9.7 67.6 all-reduce.1
where the time goes:
time: 339 us; the launch traced here: 338 us
  waiting for transfers between devices  163 us (48%)
  blocking collectives  105 us (31%)
  local copies, waits for them, and re-layouts  20.5 us (6%)
  matrix products  15 us (4%)
  other arithmetic  14.1 us (4%)
  between operations  13.5 us (4%)
  starting transfers between devices  7.34 us (2%)
    all_to_all x1, blocking collectives, on_device(): lax.all_to_all(outgoing, 'fsdp', split_axis=1, concat_axis=1, tiled=True)  105 us
    all_to_all x1, waiting for transfers between devices, on_device(): lax.all_to_all(updates, 'fsdp', split_axis=1, concat_axis=1, tiled=True)  94.5 us
    psum x1, waiting for transfers between devices, on_device(): shared = lax.psum(partial_value.astype(jnp.bfloat16), 'replica')  67.7 us
    dot_general x1, matrix products, on_device(): jnp.einsum('sij,sjk->sik', middle, right_roots, preferred_element_type=jn...  15 us
    all_to_all x1, starting transfers between devices, on_device(): lax.all_to_all(updates, 'fsdp', split_axis=1, concat_axis=1, tiled=True)  7.34 us
  transfers between devices with their start and end apart: 2, of which 2 were waited for; matrix products, arithmetic and copies ran while one was open for 1% of the time, Pallas kernels for 0%

commit v1 on v0

v1 whole, which is shorter than its diff:
```python
import jax
import jax.numpy as jnp
from jax import lax
from jax.experimental import pallas as pl
from jax.experimental.pallas import tpu as pltpu
from jax.sharding import PartitionSpec as P

EPSILON = 1e-06
MESH = pl.DeviceIdType.MESH

NY, NZ, NX = 4, 8, 4
RANKS = 64
CHIPS = NY * NZ * NX
BLOCKS = 64
HALF = BLOCKS // 2
ROWS = 16
SIDE = 1024
COLS = SIDE // NY
TILE = 256


def rem(a, b):
    return lax.rem(a, jnp.int32(b))


def div(a, b):
    return lax.div(a, jnp.int32(b))


def columns(quarter):
    return pl.ds(pl.multiple_of(quarter * COLS, COLS), COLS)


def offset(i, r, z, x):
    m, j = rem(i, NZ), div(i, NZ)
    dz = rem(3 * m, NZ)
    dx = rem(j + m, NX)
    dy = rem(div(j, NX) + m, NY)
    return rem(r + dy, NY), rem(z + dz, NZ), rem(x + dx, NX)


def kernel(holder, home, g_hbm, l_hbm, r_hbm, o, g, ta, tb, ca, cb, ra, rb, outgoing, s_ref, l_ref, r_ref, pf, d_ref,
           back, load_sem, rs_send, rs_recv, f_send, f_recv, b_send, b_recv, ag_send, ag_recv, sem_z, sem_x):
    r, f = lax.axis_index("replica"), lax.axis_index("fsdp")
    z, x, c = div(f, 8), rem(div(f, 2), NX), rem(f, 2)
    in_plane = rem(f, 8)
    slot = div(r, 2)
    active = rem(r, 2) == c
    key = 2 * f + slot

    load_g = pltpu.make_async_copy(g_hbm.at[0], g, load_sem.at[0])
    load_l = pltpu.make_async_copy(l_hbm.at[slot], l_ref, load_sem.at[1])
    load_r = pltpu.make_async_copy(r_hbm.at[slot], r_ref, load_sem.at[2])
    load_g.start()
    load_l.start()
    load_r.start()

    def z_peer(d):
        return (r, rem(z + d, NZ) * 8 + in_plane)

    def x_peer(d):
        return (r, z * 8 + rem(in_plane + d, 8))

    barrier = pltpu.get_barrier_semaphore()
    for d in range(1, NY):
        pl.semaphore_signal(barrier, inc=1, device_id=(rem(r + d, NY), f), device_id_type=MESH)

    def greet(d, _):
        pl.semaphore_signal(barrier, inc=1, device_id=z_peer(d), device_id_type=MESH)
        pl.semaphore_signal(barrier, inc=1, device_id=x_peer(d), device_id_type=MESH)
        return 0

    lax.fori_loop(1, 8, greet, 0)
    pl.semaphore_wait(barrier, 17)

    up, dn, opp = rem(r + 1, NY), rem(r + 3, NY), rem(r + 2, NY)
    low, high = pl.ds(0, HALF), pl.ds(HALF, HALF)

    def remote(n, src, dst, send, recv, plane):
        return pltpu.make_async_remote_copy(
            src_ref=src, dst_ref=dst, send_sem=send.at[n], recv_sem=recv.at[n], device_id=(plane, f), device_id_type=MESH
        )

    load_g.wait()
    far_up = remote(0, g.at[low, :, columns(opp)], ta, rs_send, rs_recv, up)
    far_dn = remote(1, g.at[high, :, columns(opp)], tb, rs_send, rs_recv, dn)
    near_up = remote(2, g.at[high, :, columns(up)], ra.at[high], rs_send, rs_recv, up)
    near_dn = remote(3, g.at[low, :, columns(dn)], rb.at[low], rs_send, rs_recv, dn)
    sum_up = remote(4, ca, ra.at[low], rs_send, rs_recv, up)
    sum_dn = remote(5, cb, rb.at[high], rs_send, rs_recv, dn)
    far_up.start()
    far_dn.start()
    near_up.start()
    near_dn.start()

    def greet_z(d, _):
        pl.semaphore_signal(sem_z, inc=1, device_id=z_peer(d), device_id_type=MESH)
        return 0

    def greet_x(d, _):
        pl.semaphore_signal(sem_x, inc=1, device_id=x_peer(d), device_id_type=MESH)
        return 0

    lax.fori_loop(1, 8, greet_z, 0)
    pl.semaphore_wait(sem_z, 7)
    lax.fori_loop(1, 8, greet_x, 0)
    pl.semaphore_wait(sem_x, 7)

    def add_up(b, _):
        ca[b] = (g[b, :, columns(up)].astype(jnp.float32) + ta[b].astype(jnp.float32)).astype(jnp.bfloat16)
        return 0

    def add_dn(b, _):
        mine = g[b + HALF, :, columns(dn)].astype(jnp.float32)
        cb[b] = (mine + tb[b].astype(jnp.float32)).astype(jnp.bfloat16)
        return 0

    far_up.wait_recv()
    lax.fori_loop(0, HALF, add_up, 0)
    sum_up.start()
    far_dn.wait_recv()
    lax.fori_loop(0, HALF, add_dn, 0)
    sum_dn.start()
    for copy in (near_up, near_dn, sum_up, sum_dn):
        copy.wait_recv()
    for copy in (far_up, far_dn, near_up, near_dn, sum_up, sum_dn):
        copy.wait_send()

    mine = columns(r)
    my_rows = pl.ds(pl.multiple_of(f * ROWS, ROWS), ROWS)

    def pack(i, rank, slot_of):
        h = holder[2 * rank + slot_of]
        total = g[h, :, mine].astype(jnp.float32) + ra[h].astype(jnp.float32) + rb[h].astype(jnp.float32)
        outgoing[i] = total.astype(jnp.bfloat16)

    def send_rows(i, plane, rank):
        return pltpu.make_async_remote_copy(
            src_ref=outgoing.at[i], dst_ref=s_ref.at[my_rows, mine], send_sem=f_send, recv_sem=f_recv,
            device_id=(plane, rank), device_id_type=MESH,
        )

    def forward(i, _):
        plane, tz, tx = offset(i, r, z, x)
        rank = tz * 8 + tx * 2 + rem(plane, 2)
        pack(i, rank, div(plane, 2))
        send_rows(i, plane, rank).start()
        return 0

    lax.fori_loop(1, CHIPS, forward, 0)
    home_rank = f - c + rem(r, 2)
    pack(0, home_rank, slot)

    @pl.when(active)
    def _():
        pltpu.make_async_copy(outgoing.at[0], s_ref.at[my_rows, mine], f_recv).start()

    @pl.when(jnp.logical_not(active))
    def _():
        send_rows(0, r, home_rank).start()
        pltpu.make_async_copy(outgoing.at[0], outgoing.at[0], f_send).wait()

    rest = outgoing.at[pl.ds(1, CHIPS - 1)]
    pltpu.make_async_copy(rest, rest, f_send).wait()

    def send_back(i, plane, rank, core):
        to = rank + core
        rows = pl.ds(pl.multiple_of(to * ROWS, ROWS), ROWS)
        return pltpu.make_async_remote_copy(
            src_ref=d_ref.at[rows, columns(plane)], dst_ref=back.at[key], send_sem=b_send, recv_sem=b_recv,
            device_id=(plane, to), device_id_type=MESH,
        )

    load_l.wait()
    load_r.wait()

    @pl.when(active)
    def _():
        pltpu.make_async_copy(s_ref, s_ref, f_recv).wait()

        def product(t, carry):
            grad_sq, pre_sq = carry
            rows = pl.ds(pl.multiple_of(t * TILE, TILE), TILE)
            middle = jnp.dot(l_ref[rows, :], s_ref[...], preferred_element_type=jnp.float32).astype(jnp.bfloat16)
            pre = jnp.dot(middle, r_ref[...], preferred_element_type=jnp.float32)
            pf[rows, :] = pre
            grad_sq = grad_sq + jnp.sum(jnp.square(s_ref[rows, :].astype(jnp.float32)), axis=0, keepdims=True)
            pre_sq = pre_sq + jnp.sum(jnp.square(pre), axis=0, keepdims=True)
            return grad_sq, pre_sq

        zero = jnp.zeros((1, SIDE), jnp.float32)
        grad_sq, pre_sq = lax.fori_loop(0, SIDE // TILE, product, (zero, zero))
        grad_ms = jnp.sum(grad_sq, axis=1, keepdims=True) / (SIDE * SIDE)
        pre_ms = jnp.sum(pre_sq, axis=1, keepdims=True) / (SIDE * SIDE)
        factor = jnp.sqrt(grad_ms) * lax.rsqrt(pre_ms + EPSILON)

        def scale(t, _):
            rows = pl.ds(pl.multiple_of(t * TILE, TILE), TILE)
            d_ref[rows, :] = (pf[rows, :] * factor).astype(jnp.bfloat16)
            return 0

        lax.fori_loop(0, SIDE // TILE, scale, 0)

        def backward(i, _):
            plane, tz, tx = offset(i, r, z, x)
            rank = tz * 8 + tx * 2
            send_back(i, plane, rank, 0).start()
            send_back(i, plane, rank, 1).start()
            return 0

        lax.fori_loop(1, CHIPS, backward, 0)
        send_back(0, r, f - c, 1 - c).start()
        pltpu.make_async_copy(d_ref.at[my_rows, mine], back.at[key], b_recv).start()
        sent = d_ref.at[pl.ds(0, SIDE - ROWS), :]
        pltpu.make_async_copy(sent, sent, b_send).wait()
        last = d_ref.at[pl.ds(0, ROWS), pl.ds(0, SIDE - COLS)]
        pltpu.make_async_copy(last, last, b_send).wait()

    pltpu.make_async_copy(back, back, b_recv).wait()

    def place(b, _):
        o[b, :, mine] = back[home[b]]
        return 0

    def spread(n, half, quarter, plane):
        part = o.at[half, :, columns(quarter)]
        return remote(n, part, part, ag_send, ag_recv, plane)

    lax.fori_loop(0, HALF, place, 0)
    low_up, low_dn = spread(0, low, r, up), spread(1, low, r, dn)
    high_up, high_dn = spread(2, high, r, up), spread(3, high, r, dn)
    low_up.start()
    lax.fori_loop(HALF, BLOCKS, place, 0)
    high_dn.start()
    high_up.start()
    low_dn.start()
    on_up, on_dn = spread(4, low, dn, up), spread(5, high, up, dn)
    low_up.wait_recv()
    on_up.start()
    high_dn.wait_recv()
    on_dn.start()
    for copy in (high_up, low_dn, on_up, on_dn):
        copy.wait_recv()
    for copy in (low_up, high_dn, high_up, low_dn, on_up, on_dn):
        copy.wait_send()


def on_device(grads, block_owner, left_roots, right_roots):
    same_owner = block_owner[:, None] == block_owner[None, :]
    positions = jnp.arange(BLOCKS, dtype=jnp.int32)
    earlier = positions[None, :] < positions[:, None]
    slot_rank = jnp.sum(jnp.logical_and(same_owner, earlier).astype(jnp.int32), axis=1)
    home = 2 * block_owner + slot_rank
    matches = home[:, None] == jnp.arange(2 * RANKS, dtype=jnp.int32)[None, :]
    holder = jnp.sum(jnp.where(matches, positions[:, None], 0), axis=0)
    bf16, f32 = jnp.bfloat16, jnp.float32
    smem, anywhere = pl.BlockSpec(memory_space=pltpu.SMEM), pl.BlockSpec(memory_space=pl.ANY)
    return pl.pallas_call(
        kernel,
        out_shape=jax.ShapeDtypeStruct((BLOCKS, ROWS, SIDE), bf16),
        in_specs=[smem, smem, anywhere, anywhere, anywhere],
        out_specs=pl.BlockSpec(memory_space=pltpu.VMEM),
        scratch_shapes=[
            pltpu.VMEM((BLOCKS, ROWS, SIDE), bf16),
            pltpu.VMEM((HALF, ROWS, COLS), bf16),
            pltpu.VMEM((HALF, ROWS, COLS), bf16),
            pltpu.VMEM((HALF, ROWS, COLS), bf16),
            pltpu.VMEM((HALF, ROWS, COLS), bf16),
            pltpu.VMEM((BLOCKS, ROWS, COLS), bf16),
            pltpu.VMEM((BLOCKS, ROWS, COLS), bf16),
            pltpu.VMEM((CHIPS, ROWS, COLS), bf16),
            pltpu.VMEM((SIDE, SIDE), bf16),
            pltpu.VMEM((SIDE, SIDE), bf16),
            pltpu.VMEM((SIDE, SIDE), bf16),
            pltpu.VMEM((SIDE, SIDE), f32),
            pltpu.VMEM((SIDE, SIDE), bf16),
            pltpu.VMEM((CHIPS, ROWS, COLS), bf16),
            pltpu.SemaphoreType.DMA((3,)),
            pltpu.SemaphoreType.DMA((6,)),
            pltpu.SemaphoreType.DMA((6,)),
            pltpu.SemaphoreType.DMA,
            pltpu.SemaphoreType.DMA,
            pltpu.SemaphoreType.DMA,
            pltpu.SemaphoreType.DMA,
            pltpu.SemaphoreType.DMA((6,)),
            pltpu.SemaphoreType.DMA((6,)),
            pltpu.SemaphoreType.REGULAR,
            pltpu.SemaphoreType.REGULAR,
        ],
        compiler_params=pltpu.CompilerParams(
            collective_id=0, has_side_effects=True, vmem_limit_bytes=40 * 1024 * 1024
        ),
        cost_estimate=pl.CostEstimate(flops=4 * SIDE**3, bytes_accessed=8 * 1024 * 1024, transcendentals=0),
    )(holder, home, grads, left_roots, right_roots)


def solution(mesh):
    in_specs = (P("replica", None, "fsdp", None), P(), P("fsdp", None, None), P("fsdp", None, None))
    return jax.shard_map(
        on_device, mesh=mesh, in_specs=in_specs, out_specs=P(None, "fsdp", None), check_vma=False
    )
```

time: 339 us -> 119 us (0.35)
  waiting for transfers between devices: 163 us -> 0 us
  Pallas kernels: 0 us -> 109 us
  blocking collectives: 105 us -> 0 us
  matrix products: 15 us -> 0 us
  between operations: 13.5 us -> 0.02 us
  local copies, waits for them, and re-layouts: 20.5 us -> 7.28 us
  other arithmetic: 14.1 us -> 1.67 us
  starting transfers between devices: 7.34 us -> 0 us
    pallas_call x0 -> x1, Pallas kernels: none -> 109 us  [on_device(): pl.pallas_call(kernel, out_shape=jax.ShapeDtypeStruct((BLOCKS, ROWS, SIDE...]
    all_to_all x1 -> x0, blocking collectives: 105 us -> none  [on_device(): lax.all_to_all(outgoing, 'fsdp', split_axis=1, concat_axis=1, tiled=True)]
    all_to_all x1 -> x0, waiting for transfers between devices: 94.5 us -> none  [on_device(): lax.all_to_all(updates, 'fsdp', split_axis=1, concat_axis=1, tiled=True)]
    psum x1 -> x0, waiting for transfers between devices: 67.7 us -> none  [on_device(): shared = lax.psum(partial_value.astype(jnp.bfloat16), 'replica')]
    dot_general x1 -> x0, matrix products: 15 us -> none  [on_device(): jnp.einsum('sij,sjk->sik', middle, right_roots, preferred_element_type=jn...]
    all_to_all x2 -> x0, local copies, waits for them, and re-layouts: 7.39 us -> none  [the longest x1 5 us: on_device(): lax.all_to_all(updates, 'fsdp', split_axis=1, concat_axis=1, tiled=True)]
    all_to_all x1 -> x0, starting transfers between devices: 7.34 us -> none  [on_device(): lax.all_to_all(updates, 'fsdp', split_axis=1, concat_axis=1, tiled=True)]
    gather x2 -> x0, local copies, waits for them, and re-layouts: 7.2 us -> none  [the longest x1 4.33 us: on_device(): jnp.take(shared, holder, axis=0)]
  transfers between devices with their start and end apart: 2 -> 0, of which waited for: 2 -> 0; matrix products, arithmetic and copies ran while one was open for 1% -> 0% of each run, Pallas kernels for 0% -> 0%
where the time goes in v1:
time: 119 us; the launch traced here: 118 us
  Pallas kernels  109 us (92%)
  local copies, waits for them, and re-layouts  7.28 us (6%)
  other arithmetic  1.67 us (1%)
    pallas_call x1, Pallas kernels, on_device(): pl.pallas_call(kernel, out_shape=jax.ShapeDtypeStruct((BLOCKS, ROWS, SIDE...  109 us
    unnamed x7, local copies, waits for them, and re-layouts  7.28 us

profile of v1, /device:TPU:1, one launch (start us, length us, event | category | flops | bytes accessed | tf_op | source)
XLA Modules:
  0.0 118.5 jit_solution(1469091672733223022)
XLA Ops:
  0.0 0.9 convert_reduce_fusion
  0.9 0.7 multiply_add_fusion.home
  1.6 0.1 select_reduce_fusion.holder
  1.7 0.0 copy-start
  1.7 2.2 %copy-done = bf16[2,1024,1024]{2,1,0:T(8,128)(2,1)S(1)} copy-done((bf16[2,1024,1024]{2,1,0:T(8,128)(2,1)S(1)}, bf16[2,1024,1024]{2,1,0:T(8,128)(2,1)}, u32[]{:S(2)}) %copy-start) | copy-done | bytes 4194328
  3.9 0.0 copy-start.1
  3.9 2.2 %copy-done.1 = bf16[2,1024,1024]{2,1,0:T(8,128)(2,1)S(1)} copy-done((bf16[2,1024,1024]{2,1,0:T(8,128)(2,1)S(1)}, bf16[2,1024,1024]{2,1,0:T(8,128)(2,1)}, u32[]{:S(2)}) %copy-start.1) | copy-done | bytes 4194328
  6.1 0.0 copy-start.2
  6.1 1.6 %copy-done.2 = bf16[1,64,16,1024]{3,2,1,0:T(8,128)(2,1)S(1)} copy-done((bf16[1,64,16,1024]{3,2,1,0:T(8,128)(2,1)S(1)}, bf16[1,64,16,1024]{3,2,1,0:T(8,128)(2,1)}, u32[]{:S(2)}) %copy-start.2) | copy-done | bytes 2097176
  7.6 109.5 %shard_map.46 = bf16[64,16,1024]{2,1,0:T(8,128)(2,1)S(1)} custom-call(s32[128]{0:T(128)S(1)} %select_reduce_fusion.holder, s32[64]{0:T(128)S(1)} %multiply_add_fusion.home, bf16[1,64,16,1024]{3,2,1,0:T(8,128)(2,1)S(1)} %copy-done.2, bf16[2,1024,1024]{2,1,0:T(8,128)(2,1)S(1)} %copy-done, bf16[2,1024,1024]{2,1,0:T(8,128)(2,1)S(1)} %copy-done.1), custom_call_target="tpu_custom_call" | custom-call | flops 4294967296 | bytes 8388608 | tf_op jit(solution)/shard_map/pallas_call | solution.py:258
  117.1 1.3 %copy.6 = bf16[64,16,1024]{2,1,0:T(8,128)(2,1)} copy(bf16[64,16,1024]{2,1,0:T(8,128)(2,1)S(1)} %shard_map.46) | data formatting | bytes 4194304
Async XLA Ops:
  1.7 2.2 %copy-start = (bf16[2,1024,1024]{2,1,0:T(8,128)(2,1)S(1)}, bf16[2,1024,1024]{2,1,0:T(8,128)(2,1)}, u32[]{:S(2)}) copy-start(bf16[2,1024,1024]{2,1,0:T(8,128)(2,1)} %l_hbm.1) | copy-start | bytes 12582916
  3.9 2.2 %copy-start.1 = (bf16[2,1024,1024]{2,1,0:T(8,128)(2,1)S(1)}, bf16[2,1024,1024]{2,1,0:T(8,128)(2,1)}, u32[]{:S(2)}) copy-start(bf16[2,1024,1024]{2,1,0:T(8,128)(2,1)} %r_hbm.1) | copy-start | bytes 12582916
  6.1 1.6 %copy-start.2 = (bf16[1,64,16,1024]{3,2,1,0:T(8,128)(2,1)S(1)}, bf16[1,64,16,1024]{3,2,1,0:T(8,128)(2,1)}, u32[]{:S(2)}) copy-start(bf16[1,64,16,1024]{3,2,1,0:T(8,128)(2,1)} %g_hbm.1) | copy-start | bytes 6291460

commit v2 on v0

v2 whole, which is shorter than its diff:
```python
import jax
import jax.numpy as jnp
from jax import lax
from jax.experimental import pallas as pl
from jax.experimental.pallas import tpu as pltpu
from jax.sharding import PartitionSpec as P

EPSILON = 1e-06
MESH = pl.DeviceIdType.MESH

NY, NZ, NX = 4, 8, 4
COLUMNS = NZ * NX
BLOCKS = 64
SHARE = BLOCKS // NY
HALF = SHARE // 2
ROWS = 16
SIDE = 1024
CHUNKS = 4
WIDTH = SIDE // CHUNKS
TILE = 512

BLOCK_OF, ENTRY_OF, CELL, PAIR, COLUMN_OF = range(5)


def rem(a, b):
    return lax.rem(a, jnp.int32(b))


def div(a, b):
    return lax.div(a, jnp.int32(b))


def chunk(k):
    return pl.ds(k * WIDTH, WIDTH)


def f32(a):
    return a.astype(jnp.float32)


def bf16(a):
    return a.astype(jnp.bfloat16)


def make_table(owner, owners, table):
    lane1 = lax.broadcasted_iota(jnp.int32, (1, 128), 1)

    def spread(b, row):
        value = owner[b]
        owners[pl.ds(b, 1), :] = jnp.full((1, 128), value, jnp.int32)
        return jnp.where(lane1 == b, value, row)

    across = lax.fori_loop(0, BLOCKS, spread, jnp.full((1, 128), 4096, jnp.int32))
    down = owners[...]
    lane = lax.broadcasted_iota(jnp.int32, (BLOCKS, 128), 1)
    sub = lax.broadcasted_iota(jnp.int32, (BLOCKS, 128), 0)
    one, zero = jnp.ones((BLOCKS, 128), jnp.int32), jnp.zeros((BLOCKS, 128), jnp.int32)
    same = down == across
    earlier = jnp.logical_and(same, lane < sub)
    place = jnp.sum(jnp.where(jnp.logical_or(across < down, earlier), one, zero), axis=1, keepdims=True)
    slot = jnp.sum(jnp.where(earlier, one, zero), axis=1, keepdims=True)
    later = jnp.logical_or(down < across, jnp.logical_and(same, sub < lane))
    place_across = jnp.sum(jnp.where(later, one, zero), axis=0, keepdims=True)
    plane, position = place & 3, place >> 2
    column = down >> 1
    entry = jnp.where(plane * SHARE + position == lane, one, zero)
    here = jnp.where(jnp.logical_and(plane == (lane >> 5), column == (lane & 31)), one, zero)
    block = jnp.sum(entry * sub, axis=0, keepdims=True)
    cell = jnp.sum(here * position, axis=0, keepdims=True)
    pair = jnp.sum(here * (2 * (down & 1) + slot), axis=0, keepdims=True)
    column_of = jnp.sum(entry * column, axis=0, keepdims=True)
    table[pl.ds(BLOCK_OF, 1), :] = block & (BLOCKS - 1)
    table[pl.ds(ENTRY_OF, 1), :] = ((place_across & 3) * SHARE + (place_across >> 2)) & (BLOCKS - 1)
    table[pl.ds(CELL, 1), :] = cell & (SHARE - 1)
    table[pl.ds(PAIR, 1), :] = pair & 3
    table[pl.ds(COLUMN_OF, 1), :] = column_of & (COLUMNS - 1)


def kernel(owner, g_hbm, l_hbm, r_hbm, o, owners, table_v, table, g, gs, ta, tb, ca, cb, ra, rb, summed, outgoing, s_ref,
           l_ref, r_ref, pf, factor_ref, d_ref, load_sem, pair_send, pair_recv, rs_send, rs_recv, f_send, f_recv, b_send,
           b_recv, ag_send, ag_recv, plane_sem, *by_chunk):
    back, fin = by_chunk[:CHUNKS], by_chunk[CHUNKS:]
    r, f = lax.axis_index("replica"), lax.axis_index("fsdp")
    z, x, c = div(f, 8), rem(div(f, 2), NX), rem(f, 2)
    in_line = rem(f, 8)
    column = div(f, 2)
    worker = rem(r, 2)
    active = worker == c
    idle = jnp.logical_not(active)
    sibling = f + 1 - 2 * c

    load_g = pltpu.make_async_copy(g_hbm.at[0], g, load_sem.at[0])
    load_g.start()

    def z_peer(d):
        return (r, rem(z + d, NZ) * 8 + in_line)

    barrier = pltpu.get_barrier_semaphore()
    for d in range(1, NY):
        pl.semaphore_signal(barrier, inc=1, device_id=(rem(r + d, NY), f), device_id_type=MESH)

    def greet(d, _):
        pl.semaphore_signal(barrier, inc=1, device_id=z_peer(d), device_id_type=MESH)
        pl.semaphore_signal(barrier, inc=1, device_id=(r, z * 8 + rem(in_line + d, 8)), device_id_type=MESH)
        return 0

    lax.fori_loop(1, 8, greet, 0)

    make_table(owner, owners, table_v)
    load_table = pltpu.make_async_copy(table_v, table, load_sem.at[1])
    load_table.start()

    pl.semaphore_wait(barrier, 17)

    def greet_plane(d, _):
        pl.semaphore_signal(plane_sem, inc=1, device_id=z_peer(d), device_id_type=MESH)
        return 0

    lax.fori_loop(1, 8, greet_plane, 0)

    own_pairs = pl.ds(2 * c, 2)
    load_l = pltpu.make_async_copy(l_hbm, l_ref.at[own_pairs], load_sem.at[2])
    load_r = pltpu.make_async_copy(r_hbm, r_ref.at[own_pairs], load_sem.at[3])

    def give(n, src, dst):
        return pltpu.make_async_remote_copy(
            src_ref=src, dst_ref=dst.at[own_pairs], send_sem=pair_send.at[n], recv_sem=pair_recv.at[n],
            device_id=(r, sibling), device_id_type=MESH,
        )

    give_l, give_r = give(0, l_hbm, l_ref), give(1, r_hbm, r_ref)

    up, dn, opp = rem(r + 1, NY), rem(r + 3, NY), rem(r + 2, NY)
    low, high = pl.ds(0, HALF), pl.ds(HALF, HALF)

    def half_of(plane, n):
        return pl.ds(plane * SHARE + n * HALF, HALF)

    def remote(n, src, dst, send, recv, plane):
        return pltpu.make_async_remote_copy(
            src_ref=src, dst_ref=dst, send_sem=send.at[n], recv_sem=recv.at[n], device_id=(plane, f), device_id_type=MESH
        )

    def sum_copies(k):
        ck, n = chunk(k), 6 * k
        return (
            remote(n, gs.at[half_of(opp, 0), :, ck], ta.at[:, :, ck], rs_send, rs_recv, up),
            remote(n + 1, gs.at[half_of(opp, 1), :, ck], tb.at[:, :, ck], rs_send, rs_recv, dn),
            remote(n + 2, gs.at[half_of(up, 1), :, ck], ra.at[high, :, ck], rs_send, rs_recv, up),
            remote(n + 3, gs.at[half_of(dn, 0), :, ck], rb.at[low, :, ck], rs_send, rs_recv, dn),
            remote(n + 4, ca.at[:, :, ck], ra.at[low, :, ck], rs_send, rs_recv, up),
            remote(n + 5, cb.at[:, :, ck], rb.at[high, :, ck], rs_send, rs_recv, dn),
        )

    sums = [sum_copies(k) for k in range(CHUNKS)]

    def sum_first(k):
        ck = chunk(k)

        def pack(e, _):
            gs[e, :, ck] = g[table[BLOCK_OF, e], :, ck]
            return 0

        lax.fori_loop(0, BLOCKS, pack, 0, unroll=4)
        for copy in sums[k][:4]:
            copy.start()

    def sum_second(k):
        ck = chunk(k)

        def add_up(i, _):
            ca[i, :, ck] = bf16(f32(gs[up * SHARE + i, :, ck]) + f32(ta[i, :, ck]))
            return 0

        def add_dn(i, _):
            cb[i, :, ck] = bf16(f32(gs[dn * SHARE + HALF + i, :, ck]) + f32(tb[i, :, ck]))
            return 0

        sums[k][0].wait_recv()
        lax.fori_loop(0, HALF, add_up, 0, unroll=4)
        sums[k][4].start()
        sums[k][1].wait_recv()
        lax.fori_loop(0, HALF, add_dn, 0, unroll=4)
        sums[k][5].start()

    def offset(n):
        m = rem(n, NZ)
        dz, dx = rem(3 * m, NZ), rem(div(n, NZ) + m, NX)
        return rem(z + dz, NZ) * NX + rem(x + dx, NX)

    def rows_of(rank):
        return pl.ds(pl.multiple_of(rank * ROWS, ROWS), ROWS)

    def forward(k):
        ck = chunk(k)
        for copy in sums[k][2:]:
            copy.wait_recv()

        def add(i, _):
            total = f32(gs[r * SHARE + i, :, ck]) + f32(ra[i, :, ck]) + f32(rb[i, :, ck])
            summed[i, :, ck] = bf16(total)
            return 0

        lax.fori_loop(0, SHARE, add, 0, unroll=4)

        def pack(q):
            outgoing[q, :, ck] = summed[table[CELL, r * COLUMNS + q], :, ck]

        def send(q):
            return pltpu.make_async_remote_copy(
                src_ref=outgoing.at[q, :, ck], dst_ref=s_ref.at[rows_of(f), ck], send_sem=f_send, recv_sem=f_recv.at[k],
                device_id=(r, 2 * q + worker), device_id_type=MESH,
            )

        def step(n, _):
            q = offset(n)
            pack(q)
            send(q).start()
            return 0

        lax.fori_loop(1, COLUMNS, step, 0)
        pack(column)

        @pl.when(active)
        def _():
            pltpu.make_async_copy(outgoing.at[column, :, ck], s_ref.at[rows_of(f), ck], f_recv.at[k]).start()

        @pl.when(idle)
        def _():
            send(column).start()

    def products(first, count):
        part = pl.ds(first * WIDTH, count * WIDTH)
        for k in range(first, first + count):
            pltpu.make_async_copy(s_ref.at[:, chunk(k)], s_ref.at[:, chunk(k)], f_recv.at[k]).wait()
        pair = table[PAIR, r * COLUMNS + column]
        last = first + count == CHUNKS

        def step(t, carry):
            grad_sq, pre_sq = carry
            rows = pl.ds(pl.multiple_of(t * TILE, TILE), TILE)
            middle = bf16(jnp.dot(l_ref[pair, rows, :], s_ref[:, part], preferred_element_type=jnp.float32))
            pre = jnp.dot(middle, r_ref[pair, part, :], preferred_element_type=jnp.float32)
            if first > 0:
                pre = pre + pf[rows, :]
            pf[rows, :] = pre
            grad_sq = grad_sq + jnp.sum(jnp.square(f32(s_ref[rows, part])), axis=0, keepdims=True)
            if last:
                pre_sq = pre_sq + jnp.sum(jnp.square(pre), axis=0, keepdims=True)
            return grad_sq, pre_sq

        zeros = (jnp.zeros((1, count * WIDTH), jnp.float32), jnp.zeros((1, SIDE), jnp.float32))
        grad_sq, pre_sq = lax.fori_loop(0, SIDE // TILE, step, zeros)
        return jnp.sum(grad_sq, axis=1, keepdims=True), jnp.sum(pre_sq, axis=1, keepdims=True)

    def backward(k):
        ck = chunk(k)

        def send(rank):
            return pltpu.make_async_remote_copy(
                src_ref=d_ref.at[rows_of(rank), ck], dst_ref=back[k].at[column], send_sem=b_send, recv_sem=b_recv.at[k],
                device_id=(r, rank), device_id_type=MESH,
            )

        @pl.when(active)
        def _():
            factor = factor_ref[...]

            def scale(t, _):
                rows = pl.ds(pl.multiple_of(t * 128, 128), 128)
                d_ref[rows, ck] = bf16(pf[rows, ck] * factor)
                return 0

            lax.fori_loop(0, SIDE // 128, scale, 0)

            def step(n, _):
                q = offset(n)
                send(2 * q).start()
                send(2 * q + 1).start()
                return 0

            lax.fori_loop(1, COLUMNS, step, 0)
            send(sibling).start()
            pltpu.make_async_copy(d_ref.at[rows_of(f), ck], back[k].at[column], b_recv.at[k]).start()

    def gather_copies(k):
        n = 6 * k

        def spread(m, plane, half, to):
            part = fin[k].at[half_of(plane, half)]
            return remote(n + m, part, part, ag_send, ag_recv, to)

        return (
            spread(0, r, 0, up), spread(1, r, 1, dn), spread(2, r, 1, up), spread(3, r, 0, dn), spread(4, dn, 0, up),
            spread(5, up, 1, dn),
        )

    gathers = [gather_copies(k) for k in range(CHUNKS)]

    def gather_first(k):
        pltpu.make_async_copy(back[k], back[k], b_recv.at[k]).wait()

        def place(i, _):
            e = r * SHARE + i
            fin[k][e] = back[k][table[COLUMN_OF, e]]
            return 0

        lax.fori_loop(0, SHARE, place, 0, unroll=4)
        for copy in gathers[k][:4]:
            copy.start()

    def gather_second(k):
        gathers[k][0].wait_recv()
        gathers[k][4].start()
        gathers[k][1].wait_recv()
        gathers[k][5].start()

    def finish(k):
        ck = chunk(k)
        for copy in gathers[k][2:]:
            copy.wait_recv()

        def place(b, _):
            o[b, :, ck] = fin[k][table[ENTRY_OF, b]]
            return 0

        lax.fori_loop(0, BLOCKS, place, 0, unroll=4)

    load_g.wait()
    load_table.wait()
    sum_first(0)

    @pl.when(active)
    def _():
        load_l.start()
        load_r.start()

    @pl.when(idle)
    def _():
        give_l.start()
        give_r.start()

    pl.semaphore_wait(plane_sem, 7)
    sum_second(0)
    sum_first(1)
    forward(0)
    sum_second(1)
    sum_first(2)
    forward(1)
    sum_second(2)
    sum_first(3)
    forward(2)
    sum_second(3)
    forward(3)

    @pl.when(active)
    def _():
        load_l.wait()
        load_r.wait()
        give_l.wait_recv()
        give_r.wait_recv()
        grad_a, _ = products(0, 2)
        grad_b, _ = products(2, 1)
        grad_c, pre_sq = products(3, 1)
        grad_ms = (grad_a + grad_b + grad_c) / (SIDE * SIDE)
        pre_ms = pre_sq / (SIDE * SIDE)
        factor_ref[...] = jnp.sqrt(grad_ms) * lax.rsqrt(pre_ms + EPSILON)

    backward(0)
    backward(1)
    gather_first(0)
    backward(2)
    gather_first(1)
    gather_second(0)
    backward(3)
    gather_first(2)
    gather_second(1)
    finish(0)
    gather_first(3)
    gather_second(2)
    finish(1)
    gather_second(3)
    finish(2)
    finish(3)

    for copies in sums + gathers:
        for copy in copies:
            copy.wait_send()

    @pl.when(active)
    def _():
        sent = outgoing.at[pl.ds(1, COLUMNS - 1)]
        pltpu.make_async_copy(sent, sent, f_send).wait()
        sent = d_ref.at[pl.ds(0, SIDE - ROWS), :]
        pltpu.make_async_copy(sent, sent, b_send).wait()

    @pl.when(idle)
    def _():
        pltpu.make_async_copy(outgoing, outgoing, f_send).wait()
        give_l.wait_send()
        give_r.wait_send()


def on_device(grads, block_owner, left_roots, right_roots):
    anywhere = pl.BlockSpec(memory_space=pltpu.HBM)
    share = pltpu.VMEM((SHARE, ROWS, SIDE), jnp.bfloat16)
    half = pltpu.VMEM((HALF, ROWS, SIDE), jnp.bfloat16)
    column = pltpu.VMEM((COLUMNS, ROWS, SIDE), jnp.bfloat16)
    whole = pltpu.VMEM((BLOCKS, ROWS, SIDE), jnp.bfloat16)
    square = pltpu.VMEM((SIDE, SIDE), jnp.bfloat16)
    roots = pltpu.VMEM((4, SIDE, SIDE), jnp.bfloat16)
    dma = pltpu.SemaphoreType.DMA
    return pl.pallas_call(
        kernel,
        out_shape=jax.ShapeDtypeStruct((BLOCKS, ROWS, SIDE), jnp.bfloat16),
        in_specs=[pl.BlockSpec(memory_space=pltpu.SMEM), anywhere, anywhere, anywhere],
        out_specs=pl.BlockSpec(memory_space=pltpu.VMEM),
        scratch_shapes=[
            pltpu.VMEM((BLOCKS, 128), jnp.int32), pltpu.VMEM((8, 128), jnp.int32), pltpu.SMEM((8, 128), jnp.int32),
            whole, whole, half, half, half, half, share, share, share, column, square, roots, roots,
            pltpu.VMEM((SIDE, SIDE), jnp.float32), pltpu.VMEM((1, 1), jnp.float32), square,
            dma((4,)), dma((2,)), dma((2,)), dma((6 * CHUNKS,)), dma((6 * CHUNKS,)), dma, dma((CHUNKS,)), dma, dma((CHUNKS,)),
            dma((6 * CHUNKS,)), dma((6 * CHUNKS,)), pltpu.SemaphoreType.REGULAR,
            *[pltpu.VMEM((COLUMNS, ROWS, WIDTH), jnp.bfloat16)] * CHUNKS,
            *[pltpu.VMEM((BLOCKS, ROWS, WIDTH), jnp.bfloat16)] * CHUNKS,
        ],
        compiler_params=pltpu.CompilerParams(
            collective_id=0, has_side_effects=True, vmem_limit_bytes=48 * 1024 * 1024
        ),
        cost_estimate=pl.CostEstimate(flops=4 * SIDE**3, bytes_accessed=12 * 1024 * 1024, transcendentals=0),
    )(block_owner, grads, left_roots, right_roots)


def solution(mesh):
    in_specs = (P("replica", None, "fsdp", None), P(), P("fsdp", None, None), P("fsdp", None, None))
    return jax.shard_map(
        on_device, mesh=mesh, in_specs=in_specs, out_specs=P(None, "fsdp", None), check_vma=False
    )
```

time: 339 us -> 87.1 us (0.26)
  waiting for transfers between devices: 163 us -> 0 us
  blocking collectives: 105 us -> 0 us
  Pallas kernels: 0 us -> 83.4 us
  local copies, waits for them, and re-layouts: 20.5 us -> 3.57 us
  matrix products: 15 us -> 0 us
  other arithmetic: 14.1 us -> 0 us
  between operations: 13.5 us -> 0.01 us
  starting transfers between devices: 7.34 us -> 0 us
    all_to_all x1 -> x0, blocking collectives: 105 us -> none  [on_device(): lax.all_to_all(outgoing, 'fsdp', split_axis=1, concat_axis=1, tiled=True)]
    all_to_all x1 -> x0, waiting for transfers between devices: 94.5 us -> none  [on_device(): lax.all_to_all(updates, 'fsdp', split_axis=1, concat_axis=1, tiled=True)]
    pallas_call x0 -> x1, Pallas kernels: none -> 83.4 us  [on_device(): pl.pallas_call(kernel, out_shape=jax.ShapeDtypeStruct((BLOCKS, ROWS, SIDE...]
    psum x1 -> x0, waiting for transfers between devices: 67.7 us -> none  [on_device(): shared = lax.psum(partial_value.astype(jnp.bfloat16), 'replica')]
    dot_general x1 -> x0, matrix products: 15 us -> none  [on_device(): jnp.einsum('sij,sjk->sik', middle, right_roots, preferred_element_type=jn...]
    all_to_all x2 -> x0, local copies, waits for them, and re-layouts: 7.39 us -> none  [the longest x1 5 us: on_device(): lax.all_to_all(updates, 'fsdp', split_axis=1, concat_axis=1, tiled=True)]
    all_to_all x1 -> x0, starting transfers between devices: 7.34 us -> none  [on_device(): lax.all_to_all(updates, 'fsdp', split_axis=1, concat_axis=1, tiled=True)]
    gather x2 -> x0, local copies, waits for them, and re-layouts: 7.2 us -> none  [the longest x1 4.33 us: on_device(): jnp.take(shared, holder, axis=0)]
  transfers between devices with their start and end apart: 2 -> 0, of which waited for: 2 -> 0; matrix products, arithmetic and copies ran while one was open for 1% -> 0% of each run, Pallas kernels for 0% -> 0%
where the time goes in v2:
time: 87.1 us; the launch traced here: 87 us
  Pallas kernels  83.4 us (96%)
  local copies, waits for them, and re-layouts  3.57 us (4%)
    pallas_call x1, Pallas kernels, on_device(): pl.pallas_call(kernel, out_shape=jax.ShapeDtypeStruct((BLOCKS, ROWS, SIDE...  83.4 us
    unnamed x5, local copies, waits for them, and re-layouts  3.57 us

profile of v2, /device:TPU:1, one launch (start us, length us, event | category | flops | bytes accessed | tf_op | source)
XLA Modules:
  0.0 87.0 jit_solution(3349713052225721789)
XLA Ops:
  0.0 0.0 copy-start
  0.0 1.6 %copy-done = bf16[1,64,16,1024]{3,2,1,0:T(8,128)(2,1)S(1)} copy-done((bf16[1,64,16,1024]{3,2,1,0:T(8,128)(2,1)S(1)}, bf16[1,64,16,1024]{3,2,1,0:T(8,128)(2,1)}, u32[]{:S(2)}) %copy-start) | copy-done | bytes 2097176
  1.6 0.0 copy-start.1
  1.6 0.7 copy-done.1
  2.2 83.4 %shard_map.46 = bf16[64,16,1024]{2,1,0:T(8,128)(2,1)S(1)} custom-call(s32[64]{0:T(128)S(1)} %copy-done.1, bf16[1,64,16,1024]{3,2,1,0:T(8,128)(2,1)S(1)} %copy-done, bf16[2,1024,1024]{2,1,0:T(8,128)(2,1)} %l_hbm.1, bf16[2,1024,1024]{2,1,0:T(8,128)(2,1)} %r_hbm.1), custom_call_target="tpu_custom_call" | custom-call | flops 4294967296 | bytes 12582912 | tf_op jit(solution)/shard_map/pallas_call | solution.py:413
  85.7 1.3 %copy.6 = bf16[64,16,1024]{2,1,0:T(8,128)(2,1)} copy(bf16[64,16,1024]{2,1,0:T(8,128)(2,1)S(1)} %shard_map.46) | data formatting | bytes 4194304
Async XLA Ops:
  0.0 1.6 %copy-start = (bf16[1,64,16,1024]{3,2,1,0:T(8,128)(2,1)S(1)}, bf16[1,64,16,1024]{3,2,1,0:T(8,128)(2,1)}, u32[]{:S(2)}) copy-start(bf16[1,64,16,1024]{3,2,1,0:T(8,128)(2,1)} %g_hbm.1) | copy-start | bytes 6291460
  1.6 0.7 copy-start.1

commit v3 on v2

--- a/solution.py
+++ b/solution.py
@@ -15,8 +15,9 @@
 HALF = SHARE // 2
 ROWS = 16
 SIDE = 1024
-CHUNKS = 4
-WIDTH = SIDE // CHUNKS
+OUT = (256, 256, 256, 256)
+BACK = (256, 256, 256, 256)
+PARTS = ((0, 2), (2, 1), (3, 1))
 TILE = 512
 
 BLOCK_OF, ENTRY_OF, CELL, PAIR, COLUMN_OF = range(5)
@@ -30,8 +31,8 @@
     return lax.div(a, jnp.int32(b))
 
 
-def chunk(k):
-    return pl.ds(k * WIDTH, WIDTH)
+def chunk(widths, k, count=1):
+    return pl.ds(sum(widths[:k]), sum(widths[k : k + count]))
 
 
 def f32(a):
@@ -78,8 +79,8 @@
 
 def kernel(owner, g_hbm, l_hbm, r_hbm, o, owners, table_v, table, g, gs, ta, tb, ca, cb, ra, rb, summed, outgoing, s_ref,
            l_ref, r_ref, pf, factor_ref, d_ref, load_sem, pair_send, pair_recv, rs_send, rs_recv, f_send, f_recv, b_send,
-           b_recv, ag_send, ag_recv, plane_sem, *by_chunk):
-    back, fin = by_chunk[:CHUNKS], by_chunk[CHUNKS:]
+           b_recv, d_send, d_recv, ag_send, ag_recv, plane_sem, *by_chunk):
+    back, fin = by_chunk[: len(BACK)], by_chunk[len(BACK) :]
     r, f = lax.axis_index("replica"), lax.axis_index("fsdp")
     z, x, c = div(f, 8), rem(div(f, 2), NX), rem(f, 2)
     in_line = rem(f, 8)
@@ -142,7 +143,7 @@
         )
 
     def sum_copies(k):
-        ck, n = chunk(k), 6 * k
+        ck, n = chunk(OUT, k), 6 * k
         return (
             remote(n, gs.at[half_of(opp, 0), :, ck], ta.at[:, :, ck], rs_send, rs_recv, up),
             remote(n + 1, gs.at[half_of(opp, 1), :, ck], tb.at[:, :, ck], rs_send, rs_recv, dn),
@@ -152,10 +153,10 @@
             remote(n + 5, cb.at[:, :, ck], rb.at[high, :, ck], rs_send, rs_recv, dn),
         )
 
-    sums = [sum_copies(k) for k in range(CHUNKS)]
+    sums = [sum_copies(k) for k in range(len(OUT))]
 
     def sum_first(k):
-        ck = chunk(k)
+        ck = chunk(OUT, k)
 
         def pack(e, _):
             gs[e, :, ck] = g[table[BLOCK_OF, e], :, ck]
@@ -166,7 +167,7 @@
             copy.start()
 
     def sum_second(k):
-        ck = chunk(k)
+        ck = chunk(OUT, k)
 
         def add_up(i, _):
             ca[i, :, ck] = bf16(f32(gs[up * SHARE + i, :, ck]) + f32(ta[i, :, ck]))
@@ -184,15 +185,16 @@
         sums[k][5].start()
 
     def offset(n):
-        m = rem(n, NZ)
-        dz, dx = rem(3 * m, NZ), rem(div(n, NZ) + m, NX)
-        return rem(z + dz, NZ) * NX + rem(x + dx, NX)
+        def step(i, size):
+            return rem(size // 2 + div(i + 1, 2) * (1 - 2 * rem(i, 2)), size)
+
+        return rem(z + step(div(n, NX), NZ), NZ) * NX + rem(x + step(rem(n, NX), NX), NX)
 
     def rows_of(rank):
         return pl.ds(pl.multiple_of(rank * ROWS, ROWS), ROWS)
 
     def forward(k):
-        ck = chunk(k)
+        ck = chunk(OUT, k)
         for copy in sums[k][2:]:
             copy.wait_recv()
 
@@ -218,7 +220,7 @@
             send(q).start()
             return 0
 
-        lax.fori_loop(1, COLUMNS, step, 0)
+        lax.fori_loop(0, COLUMNS - 1, step, 0)
         pack(column)
 
         @pl.when(active)
@@ -230,11 +232,11 @@
             send(column).start()
 
     def products(first, count):
-        part = pl.ds(first * WIDTH, count * WIDTH)
+        part = chunk(OUT, first, count)
         for k in range(first, first + count):
-            pltpu.make_async_copy(s_ref.at[:, chunk(k)], s_ref.at[:, chunk(k)], f_recv.at[k]).wait()
+            pltpu.make_async_copy(s_ref.at[:, chunk(OUT, k)], s_ref.at[:, chunk(OUT, k)], f_recv.at[k]).wait()
         pair = table[PAIR, r * COLUMNS + column]
-        last = first + count == CHUNKS
+        last = first + count == len(OUT)
 
         def step(t, carry):
             grad_sq, pre_sq = carry
@@ -249,39 +251,46 @@
                 pre_sq = pre_sq + jnp.sum(jnp.square(pre), axis=0, keepdims=True)
             return grad_sq, pre_sq
 
-        zeros = (jnp.zeros((1, count * WIDTH), jnp.float32), jnp.zeros((1, SIDE), jnp.float32))
+        zeros = (jnp.zeros((1, part.size), jnp.float32), jnp.zeros((1, SIDE), jnp.float32))
         grad_sq, pre_sq = lax.fori_loop(0, SIDE // TILE, step, zeros)
         return jnp.sum(grad_sq, axis=1, keepdims=True), jnp.sum(pre_sq, axis=1, keepdims=True)
 
+    def hand_over(k):
+        rows = d_ref.at[:, 1 - worker, :, chunk(BACK, k)]
+        return pltpu.make_async_remote_copy(
+            src_ref=rows, dst_ref=rows, send_sem=d_send.at[k], recv_sem=d_recv.at[k], device_id=(r, sibling),
+            device_id_type=MESH,
+        )
+
     def backward(k):
-        ck = chunk(k)
-
-        def send(rank):
-            return pltpu.make_async_remote_copy(
-                src_ref=d_ref.at[rows_of(rank), ck], dst_ref=back[k].at[column], send_sem=b_send, recv_sem=b_recv.at[k],
-                device_id=(r, rank), device_id_type=MESH,
-            )
+        ck = chunk(BACK, k)
 
         @pl.when(active)
         def _():
             factor = factor_ref[...]
 
             def scale(t, _):
-                rows = pl.ds(pl.multiple_of(t * 128, 128), 128)
-                d_ref[rows, ck] = bf16(pf[rows, ck] * factor)
+                part = pf[pl.ds(pl.multiple_of(t * 128, 128), 128), ck] * factor
+                d_ref[pl.ds(t * 4, 4), :, :, ck] = bf16(part).reshape(4, 2, ROWS, BACK[k])
                 return 0
 
             lax.fori_loop(0, SIDE // 128, scale, 0)
-
-            def step(n, _):
-                q = offset(n)
-                send(2 * q).start()
-                send(2 * q + 1).start()
-                return 0
-
-            lax.fori_loop(1, COLUMNS, step, 0)
-            send(sibling).start()
-            pltpu.make_async_copy(d_ref.at[rows_of(f), ck], back[k].at[column], b_recv.at[k]).start()
+            hand_over(k).start()
+
+        @pl.when(idle)
+        def _():
+            hand_over(k).wait_recv()
+
+        def step(n, _):
+            q = offset(n)
+            pltpu.make_async_remote_copy(
+                src_ref=d_ref.at[q, c, :, ck], dst_ref=back[k].at[column], send_sem=b_send, recv_sem=b_recv.at[k],
+                device_id=(r, 2 * q + c), device_id_type=MESH,
+            ).start()
+            return 0
+
+        lax.fori_loop(0, COLUMNS - 1, step, 0)
+        pltpu.make_async_copy(d_ref.at[column, c, :, ck], back[k].at[column], b_recv.at[k]).start()
 
     def gather_copies(k):
         n = 6 * k
@@ -295,7 +304,7 @@
             spread(5, up, 1, dn),
         )
 
-    gathers = [gather_copies(k) for k in range(CHUNKS)]
+    gathers = [gather_copies(k) for k in range(len(BACK))]
 
     def gather_first(k):
         pltpu.make_async_copy(back[k], back[k], b_recv.at[k]).wait()
@@ -316,7 +325,7 @@
         gathers[k][5].start()
 
     def finish(k):
-        ck = chunk(k)
+        ck = chunk(BACK, k)
         for copy in gathers[k][2:]:
             copy.wait_recv()
 
@@ -340,18 +349,15 @@
         give_l.start()
         give_r.start()
 
-    pl.semaphore_wait(plane_sem, 7)
     sum_second(0)
     sum_first(1)
-    forward(0)
-    sum_second(1)
-    sum_first(2)
-    forward(1)
-    sum_second(2)
-    sum_first(3)
-    forward(2)
-    sum_second(3)
-    forward(3)
+    pl.semaphore_wait(plane_sem, 7)
+    for k in range(len(OUT)):
+        forward(k)
+        if k + 1 < len(OUT):
+            sum_second(k + 1)
+        if k + 2 < len(OUT):
+            sum_first(k + 2)
 
     @pl.when(active)
     def _():
@@ -359,40 +365,36 @@
         load_r.wait()
         give_l.wait_recv()
         give_r.wait_recv()
-        grad_a, _ = products(0, 2)
-        grad_b, _ = products(2, 1)
-        grad_c, pre_sq = products(3, 1)
-        grad_ms = (grad_a + grad_b + grad_c) / (SIDE * SIDE)
+        grad_ms, pre_sq = jnp.zeros((1, 1), jnp.float32), None
+        for first, count in PARTS:
+            grad_sq, pre_sq = products(first, count)
+            grad_ms = grad_ms + grad_sq / (SIDE * SIDE)
         pre_ms = pre_sq / (SIDE * SIDE)
         factor_ref[...] = jnp.sqrt(grad_ms) * lax.rsqrt(pre_ms + EPSILON)
 
-    backward(0)
-    backward(1)
-    gather_first(0)
-    backward(2)
-    gather_first(1)
-    gather_second(0)
-    backward(3)
-    gather_first(2)
-    gather_second(1)
-    finish(0)
-    gather_first(3)
-    gather_second(2)
-    finish(1)
-    gather_second(3)
-    finish(2)
-    finish(3)
+    for k in range(len(BACK) + 3):
+        if k < len(BACK):
+            backward(k)
+        if 1 <= k <= len(BACK):
+            gather_first(k - 1)
+        if 2 <= k <= len(BACK) + 1:
+            gather_second(k - 2)
+        if k >= 3:
+            finish(k - 3)
 
     for copies in sums + gathers:
         for copy in copies:
             copy.wait_send()
+
+    sent = d_ref.at[pl.ds(1, COLUMNS - 1), 0]
+    pltpu.make_async_copy(sent, sent, b_send).wait()
 
     @pl.when(active)
     def _():
         sent = outgoing.at[pl.ds(1, COLUMNS - 1)]
         pltpu.make_async_copy(sent, sent, f_send).wait()
-        sent = d_ref.at[pl.ds(0, SIDE - ROWS), :]
-        pltpu.make_async_copy(sent, sent, b_send).wait()
+        for k in range(len(BACK)):
+            hand_over(k).wait_send()
 
     @pl.when(idle)
     def _():
@@ -418,14 +420,14 @@
         scratch_shapes=[
             pltpu.VMEM((BLOCKS, 128), jnp.int32), pltpu.VMEM((8, 128), jnp.int32), pltpu.SMEM((8, 128), jnp.int32),
             whole, whole, half, half, half, half, share, share, share, column, square, roots, roots,
-            pltpu.VMEM((SIDE, SIDE), jnp.float32), pltpu.VMEM((1, 1), jnp.float32), square,
-            dma((4,)), dma((2,)), dma((2,)), dma((6 * CHUNKS,)), dma((6 * CHUNKS,)), dma, dma((CHUNKS,)), dma, dma((CHUNKS,)),
-            dma((6 * CHUNKS,)), dma((6 * CHUNKS,)), pltpu.SemaphoreType.REGULAR,
-            *[pltpu.VMEM((COLUMNS, ROWS, WIDTH), jnp.bfloat16)] * CHUNKS,
-            *[pltpu.VMEM((BLOCKS, ROWS, WIDTH), jnp.bfloat16)] * CHUNKS,
+            pltpu.VMEM((SIDE, SIDE), jnp.float32), pltpu.VMEM((1, 1), jnp.float32), pltpu.VMEM((COLUMNS, 2, ROWS, SIDE), jnp.bfloat16),
+            dma((4,)), dma((2,)), dma((2,)), dma((6 * len(OUT),)), dma((6 * len(OUT),)), dma, dma((len(OUT),)), dma, dma((len(BACK),)),
+            dma((len(BACK),)), dma((len(BACK),)), dma((6 * len(BACK),)), dma((6 * len(BACK),)), pltpu.SemaphoreType.REGULAR,
+            *[pltpu.VMEM((COLUMNS, ROWS, width), jnp.bfloat16) for width in BACK],
+            *[pltpu.VMEM((BLOCKS, ROWS, width), jnp.bfloat16) for width in BACK],
         ],
         compiler_params=pltpu.CompilerParams(
-            collective_id=0, has_side_effects=True, vmem_limit_bytes=48 * 1024 * 1024
+            collective_id=0, has_side_effects=True, vmem_limit_bytes=51 * 1024 * 1024
         ),
         cost_estimate=pl.CostEstimate(flops=4 * SIDE**3, bytes_accessed=12 * 1024 * 1024, transcendentals=0),
     )(block_owner, grads, left_roots, right_roots)

time: 87.1 us -> 82.3 us (0.945)
  Pallas kernels: 83.4 us -> 80 us
  local copies, waits for them, and re-layouts: 3.57 us -> 1.98 us
    pallas_call x1, Pallas kernels: 83.4 us -> 80 us  [on_device(): pl.pallas_call(kernel, out_shape=jax.ShapeDtypeStruct((BLOCKS, ROWS, SIDE...]
    unnamed x5 -> x3, local copies, waits for them, and re-layouts: 3.57 us -> 1.98 us
where the time goes in v3:
time: 82.3 us; the launch traced here: 82 us
  Pallas kernels  80 us (97%)
  local copies, waits for them, and re-layouts  1.98 us (2%)
    pallas_call x1, Pallas kernels, on_device(): pl.pallas_call(kernel, out_shape=jax.ShapeDtypeStruct((BLOCKS, ROWS, SIDE...  80 us
    unnamed x3, local copies, waits for them, and re-layouts  1.98 us

profile of v3, /device:TPU:1, one launch (start us, length us, event | category | flops | bytes accessed | tf_op | source)
XLA Modules:
  0.0 82.0 jit_solution(8297922093152670905)
XLA Ops:
  0.0 0.0 copy-start
  0.0 0.7 copy-done
  0.7 80.0 %shard_map.46 = bf16[64,16,1024]{2,1,0:T(8,128)(2,1)S(1)} custom-call(s32[64]{0:T(128)S(1)} %copy-done, bf16[1,64,16,1024]{3,2,1,0:T(8,128)(2,1)} %g_hbm.1, bf16[2,1024,1024]{2,1,0:T(8,128)(2,1)} %l_hbm.1, bf16[2,1024,1024]{2,1,0:T(8,128)(2,1)} %r_hbm.1), custom_call_target="tpu_custom_call" | custom-call | flops 4294967296 | bytes 12582912 | tf_op jit(solution)/shard_map/pallas_call | solution.py:415
  80.7 1.3 %copy.6 = bf16[64,16,1024]{2,1,0:T(8,128)(2,1)} copy(bf16[64,16,1024]{2,1,0:T(8,128)(2,1)S(1)} %shard_map.46) | data formatting | bytes 4194304
Async XLA Ops:
  0.0 0.7 copy-start

commit v4 on v3

--- a/solution.py
+++ b/solution.py
@@ -18,7 +18,7 @@
 OUT = (256, 256, 256, 256)
 BACK = (256, 256, 256, 256)
 PARTS = ((0, 2), (2, 1), (3, 1))
-TILE = 512
+TILE = 1024
 
 BLOCK_OF, ENTRY_OF, CELL, PAIR, COLUMN_OF = range(5)
 
@@ -111,14 +111,6 @@
     load_table = pltpu.make_async_copy(table_v, table, load_sem.at[1])
     load_table.start()
 
-    pl.semaphore_wait(barrier, 17)
-
-    def greet_plane(d, _):
-        pl.semaphore_signal(plane_sem, inc=1, device_id=z_peer(d), device_id_type=MESH)
-        return 0
-
-    lax.fori_loop(1, 8, greet_plane, 0)
-
     own_pairs = pl.ds(2 * c, 2)
     load_l = pltpu.make_async_copy(l_hbm, l_ref.at[own_pairs], load_sem.at[2])
     load_r = pltpu.make_async_copy(r_hbm, r_ref.at[own_pairs], load_sem.at[3])
@@ -155,7 +147,7 @@
 
     sums = [sum_copies(k) for k in range(len(OUT))]
 
-    def sum_first(k):
+    def sum_pack(k):
         ck = chunk(OUT, k)
 
         def pack(e, _):
@@ -163,7 +155,18 @@
             return 0
 
         lax.fori_loop(0, BLOCKS, pack, 0, unroll=4)
+
+    def sum_first(k):
         for copy in sums[k][:4]:
+            copy.start()
+
+    def sum_far(k):
+        sum_pack(k)
+        for copy in sums[k][:2]:
+            copy.start()
+
+    def sum_near(k):
+        for copy in sums[k][2:4]:
             copy.start()
 
     def sum_second(k):
@@ -274,7 +277,7 @@
                 d_ref[pl.ds(t * 4, 4), :, :, ck] = bf16(part).reshape(4, 2, ROWS, BACK[k])
                 return 0
 
-            lax.fori_loop(0, SIDE // 128, scale, 0)
+            lax.fori_loop(0, SIDE // 128, scale, 0, unroll=4)
             hand_over(k).start()
 
         @pl.when(idle)
@@ -337,7 +340,15 @@
 
     load_g.wait()
     load_table.wait()
+    sum_pack(0)
+    pl.semaphore_wait(barrier, 17)
     sum_first(0)
+
+    def greet_plane(d, _):
+        pl.semaphore_signal(plane_sem, inc=1, device_id=z_peer(d), device_id_type=MESH)
+        return 0
+
+    lax.fori_loop(1, 8, greet_plane, 0)
 
     @pl.when(active)
     def _():
@@ -350,14 +361,20 @@
         give_r.start()
 
     sum_second(0)
+    sum_pack(1)
     sum_first(1)
     pl.semaphore_wait(plane_sem, 7)
-    for k in range(len(OUT)):
-        forward(k)
-        if k + 1 < len(OUT):
-            sum_second(k + 1)
-        if k + 2 < len(OUT):
-            sum_first(k + 2)
+    forward(0)
+    sum_second(1)
+    sum_pack(2)
+    sum_first(2)
+    forward(1)
+    sum_second(2)
+    sum_pack(3)
+    sum_first(3)
+    forward(2)
+    sum_second(3)
+    forward(3)
 
     @pl.when(active)
     def _():

time: 82.3 us -> 80.8 us (0.982)
  Pallas kernels: 80 us -> 78.6 us
    pallas_call x1, Pallas kernels: 80 us -> 78.6 us  [on_device(): pl.pallas_call(kernel, out_shape=jax.ShapeDtypeStruct((BLOCKS, ROWS, SIDE...]
where the time goes in v4:
time: 80.8 us; the launch traced here: 80.5 us
  Pallas kernels  78.6 us (97%)
  local copies, waits for them, and re-layouts  1.98 us (2%)
    pallas_call x1, Pallas kernels, on_device(): pl.pallas_call(kernel, out_shape=jax.ShapeDtypeStruct((BLOCKS, ROWS, SIDE...  78.6 us
    unnamed x3, local copies, waits for them, and re-layouts  1.98 us

profile of v4, /device:TPU:1, one launch (start us, length us, event | category | flops | bytes accessed | tf_op | source)
XLA Modules:
  0.0 80.5 jit_solution(9323689997620411104)
XLA Ops:
  0.0 0.0 copy-start
  0.0 0.7 copy-done
  0.7 78.6 %shard_map.46 = bf16[64,16,1024]{2,1,0:T(8,128)(2,1)S(1)} custom-call(s32[64]{0:T(128)S(1)} %copy-done, bf16[1,64,16,1024]{3,2,1,0:T(8,128)(2,1)} %g_hbm.1, bf16[2,1024,1024]{2,1,0:T(8,128)(2,1)} %l_hbm.1, bf16[2,1024,1024]{2,1,0:T(8,128)(2,1)} %r_hbm.1), custom_call_target="tpu_custom_call" | custom-call | flops 4294967296 | bytes 12582912 | tf_op jit(solution)/shard_map/pallas_call | solution.py:432
  79.2 1.3 %copy.6 = bf16[64,16,1024]{2,1,0:T(8,128)(2,1)} copy(bf16[64,16,1024]{2,1,0:T(8,128)(2,1)S(1)} %shard_map.46) | data formatting | bytes 4194304
Async XLA Ops:
  0.0 0.7 copy-start

commit v5 on v4

--- a/solution.py
+++ b/solution.py
@@ -223,7 +223,7 @@
             send(q).start()
             return 0
 
-        lax.fori_loop(0, COLUMNS - 1, step, 0)
+        lax.fori_loop(0, COLUMNS - 1, step, 0, unroll=True)
         pack(column)
 
         @pl.when(active)
@@ -292,7 +292,7 @@
             ).start()
             return 0
 
-        lax.fori_loop(0, COLUMNS - 1, step, 0)
+        lax.fori_loop(0, COLUMNS - 1, step, 0, unroll=True)
         pltpu.make_async_copy(d_ref.at[column, c, :, ck], back[k].at[column], b_recv.at[k]).start()
 
     def gather_copies(k):

time: 80.8 us -> 80.5 us (level)
  no operation moved by 1% of the time
where the time goes in v5:
time: 80.5 us; the launch traced here: 80.4 us
  Pallas kernels  78.4 us (97%)
  local copies, waits for them, and re-layouts  1.98 us (2%)
    pallas_call x1, Pallas kernels, on_device(): pl.pallas_call(kernel, out_shape=jax.ShapeDtypeStruct((BLOCKS, ROWS, SIDE...  78.4 us
    unnamed x3, local copies, waits for them, and re-layouts  1.98 us

profile of v5, /device:TPU:1, one launch (start us, length us, event | category | flops | bytes accessed | tf_op | source)
XLA Modules:
  0.0 80.4 jit_solution(9254868083821653906)
XLA Ops:
  0.0 0.0 copy-start
  0.0 0.7 copy-done
  0.7 78.4 %shard_map.46 = bf16[64,16,1024]{2,1,0:T(8,128)(2,1)S(1)} custom-call(s32[64]{0:T(128)S(1)} %copy-done, bf16[1,64,16,1024]{3,2,1,0:T(8,128)(2,1)} %g_hbm.1, bf16[2,1024,1024]{2,1,0:T(8,128)(2,1)} %l_hbm.1, bf16[2,1024,1024]{2,1,0:T(8,128)(2,1)} %r_hbm.1), custom_call_target="tpu_custom_call" | custom-call | flops 4294967296 | bytes 12582912 | tf_op jit(solution)/shard_map/pallas_call | solution.py:432
  79.1 1.3 %copy.6 = bf16[64,16,1024]{2,1,0:T(8,128)(2,1)} copy(bf16[64,16,1024]{2,1,0:T(8,128)(2,1)S(1)} %shard_map.46) | data formatting | bytes 4194304
Async XLA Ops:
  0.0 0.7 copy-start

commit v6 on v5

--- a/solution.py
+++ b/solution.py
@@ -154,7 +154,7 @@
             gs[e, :, ck] = g[table[BLOCK_OF, e], :, ck]
             return 0
 
-        lax.fori_loop(0, BLOCKS, pack, 0, unroll=4)
+        lax.fori_loop(0, BLOCKS, pack, 0, unroll=8)
 
     def sum_first(k):
         for copy in sums[k][:4]:
@@ -181,10 +181,10 @@
             return 0
 
         sums[k][0].wait_recv()
-        lax.fori_loop(0, HALF, add_up, 0, unroll=4)
+        lax.fori_loop(0, HALF, add_up, 0, unroll=8)
         sums[k][4].start()
         sums[k][1].wait_recv()
-        lax.fori_loop(0, HALF, add_dn, 0, unroll=4)
+        lax.fori_loop(0, HALF, add_dn, 0, unroll=8)
         sums[k][5].start()
 
     def offset(n):
@@ -206,7 +206,7 @@
             summed[i, :, ck] = bf16(total)
             return 0
 
-        lax.fori_loop(0, SHARE, add, 0, unroll=4)
+        lax.fori_loop(0, SHARE, add, 0, unroll=8)
 
         def pack(q):
             outgoing[q, :, ck] = summed[table[CELL, r * COLUMNS + q], :, ck]
@@ -277,7 +277,7 @@
                 d_ref[pl.ds(t * 4, 4), :, :, ck] = bf16(part).reshape(4, 2, ROWS, BACK[k])
                 return 0
 
-            lax.fori_loop(0, SIDE // 128, scale, 0, unroll=4)
+            lax.fori_loop(0, SIDE // 128, scale, 0, unroll=8)
             hand_over(k).start()
 
         @pl.when(idle)
@@ -317,7 +317,7 @@
             fin[k][e] = back[k][table[COLUMN_OF, e]]
             return 0
 
-        lax.fori_loop(0, SHARE, place, 0, unroll=4)
+        lax.fori_loop(0, SHARE, place, 0, unroll=8)
         for copy in gathers[k][:4]:
             copy.start()
 
@@ -336,7 +336,7 @@
             o[b, :, ck] = fin[k][table[ENTRY_OF, b]]
             return 0
 
-        lax.fori_loop(0, BLOCKS, place, 0, unroll=4)
+        lax.fori_loop(0, BLOCKS, place, 0, unroll=8)
 
     load_g.wait()
     load_table.wait()
@@ -360,8 +360,8 @@
         give_l.start()
         give_r.start()
 
+    sum_pack(1)
     sum_second(0)
-    sum_pack(1)
     sum_first(1)
     pl.semaphore_wait(plane_sem, 7)
     forward(0)

time: 80.5 us -> 80.4 us (level)
  no operation moved by 1% of the time
where the time goes in v6:
time: 80.4 us; the launch traced here: 80.2 us
  Pallas kernels  78.2 us (97%)
  local copies, waits for them, and re-layouts  1.98 us (2%)
    pallas_call x1, Pallas kernels, on_device(): pl.pallas_call(kernel, out_shape=jax.ShapeDtypeStruct((BLOCKS, ROWS, SIDE...  78.2 us
    unnamed x3, local copies, waits for them, and re-layouts  1.98 us

profile of v6, /device:TPU:1, one launch (start us, length us, event | category | flops | bytes accessed | tf_op | source)
XLA Modules:
  0.0 80.2 jit_solution(8442216326218457396)
XLA Ops:
  0.0 0.0 copy-start
  0.0 0.7 copy-done
  0.7 78.2 %shard_map.46 = bf16[64,16,1024]{2,1,0:T(8,128)(2,1)S(1)} custom-call(s32[64]{0:T(128)S(1)} %copy-done, bf16[1,64,16,1024]{3,2,1,0:T(8,128)(2,1)} %g_hbm.1, bf16[2,1024,1024]{2,1,0:T(8,128)(2,1)} %l_hbm.1, bf16[2,1024,1024]{2,1,0:T(8,128)(2,1)} %r_hbm.1), custom_call_target="tpu_custom_call" | custom-call | flops 4294967296 | bytes 12582912 | tf_op jit(solution)/shard_map/pallas_call | solution.py:432
  78.9 1.3 %copy.6 = bf16[64,16,1024]{2,1,0:T(8,128)(2,1)} copy(bf16[64,16,1024]{2,1,0:T(8,128)(2,1)S(1)} %shard_map.46) | data formatting | bytes 4194304
Async XLA Ops:
  0.0 0.7 copy-start
